TPU v7x, 256 devices: a whole 4x4x8 slice. The times are simulated.
256 devices in a mesh: lat: 8 (over y, x_lo), lon: 32 (over x_hi, z, core).
Axes of the slice: x: 4 (x_hi: 2, x_lo: 2; x = x_hi * 2 + x_lo), y: 4, z: 8, core: 2. Of those that a mesh axis runs over, the one named last changes fastest.
Arguments:
- input_field: bfloat16 [256, 2048, 256], P('lat', 'lon'), may hold values from -6 to 6
- cotangent: bfloat16 [256, 2048, 256], P('lat', 'lon'), may hold values from -6 to 6
- weight: bfloat16 [9, 256, 256], replicated, may hold values from -0.125 to 0.125
- basis_values: bfloat16 [256, 3, 65], replicated, may hold values from -3 to 3
- basis_index: int32 [256, 3, 65], replicated, may hold values from 0 to 9
- halo_width: int32 [256], replicated, may hold values from 1 to 32, as said below
Outputs:
- input_grad: float32 [256, 2048, 256], P('lat', 'lon')
- weight_grad: float32 [9, 256, 256], P(None, 'lat')
Inputs may be any that keep to these rules, and one draw needn't show every extreme that they name: `basis_index`: value 9 marks an offset outside the filter's support. `halo_width`: rows 0 and 255 have width 32.
All inputs are finite; a program needn't handle non-finite values.
Results may differ from a plain program's by a relative error of at most 0.0042.
Values may be sent and summed in bfloat16 or wider, within the bound.
A program may use at most 192 MiB of HBM per device.

v0:
```python
import math

import jax
import jax.numpy as jnp
from jax import lax
from jax.sharding import PartitionSpec as P

K = 9
HALO = 32


def extended(block, sides, width, periodic):
    for axis, dim in sides:
        count = lax.axis_size(axis)
        forward = [(i, i + 1) for i in range(count - 1)]
        if periodic:
            forward.append((count - 1, 0))
        backward = [(target, source) for source, target in forward]
        low = lax.ppermute(
            lax.slice_in_dim(block, block.shape[dim] - width, None, axis=dim), axis, forward
        )
        high = lax.ppermute(lax.slice_in_dim(block, 0, width, axis=dim), axis, backward)
        block = jnp.concatenate([low, block, high], axis=dim)
    return block


def make_filter(basis_values, basis_index, halo_width):
    offsets = jnp.arange(2 * HALO + 1, dtype=jnp.int32) - HALO
    chosen = basis_index[:, None, :, :] == jnp.arange(K, dtype=jnp.int32)[None, :, None, None]
    inside = jnp.abs(offsets)[None, None, None, :] <= halo_width[:, None, None, None]
    zeros = jnp.zeros((), jnp.bfloat16)
    return jnp.where(chosen & inside, basis_values[:, None, :, :], zeros)


def shards(input_field, cotangent, weight, basis_values, basis_index, halo_width):
    lat_rows = input_field.shape[0]
    lon_cols = input_field.shape[1]
    chans = input_field.shape[2]
    ext_cols = lon_cols + 2 * HALO
    first_row = lax.axis_index("lat") * lat_rows
    values_pad = jnp.pad(basis_values, ((1, 1), (0, 0), (0, 0)))
    index_pad = jnp.pad(basis_index, ((1, 1), (0, 0), (0, 0)), constant_values=K)
    widths_pad = jnp.pad(halo_width, (1, 1))
    filters_ext = make_filter(
        lax.dynamic_slice_in_dim(values_pad, first_row, lat_rows + 2, 0),
        lax.dynamic_slice_in_dim(index_pad, first_row, lat_rows + 2, 0),
        lax.dynamic_slice_in_dim(widths_pad, first_row, lat_rows + 2, 0),
    )
    filters_own = filters_ext[1:-1]
    global_rows = (first_row + jnp.arange(lat_rows, dtype=jnp.int32)).astype(jnp.float32)
    nlat_total = lat_rows * lax.axis_size("lat")
    nlon_total = lon_cols * lax.axis_size("lon")
    area_weight = jnp.pi / 2 * jnp.sin(jnp.pi * (global_rows + 0.5) / nlat_total)
    out_grad = (area_weight[:, None, None] * cotangent.astype(jnp.float32)).astype(jnp.bfloat16)
    taps = jnp.arange(2 * HALO + 1, dtype=jnp.int32)
    col_out = jnp.arange(lon_cols, dtype=jnp.int32)
    col_ext = jnp.arange(ext_cols, dtype=jnp.int32)
    forward_table = ((col_ext[None, :] - col_out[:, None])[None] == taps[:, None, None]).astype(
        jnp.bfloat16
    )
    banded = jnp.einsum(
        "ikrd,dje->ikrje", filters_own, forward_table, preferred_element_type=jnp.float32
    ).astype(jnp.bfloat16)
    widened = extended(input_field, (("lon", 1),), HALO, True)
    field_ext = extended(widened, (("lat", 0),), 1, False)
    row_stack = jnp.stack([field_ext[row_r : row_r + lat_rows] for row_r in range(3)], axis=1)
    basis_out = jnp.einsum(
        "ikrje,irec->ikjc", banded, row_stack, preferred_element_type=jnp.float32
    ).astype(jnp.bfloat16)
    partial_weight = jnp.einsum(
        "ikjc,ijo->kco", basis_out, out_grad, preferred_element_type=jnp.float32
    )
    grad_basis = jnp.einsum(
        "ijo,kco->ikjc", out_grad, weight, preferred_element_type=jnp.float32
    ).astype(jnp.bfloat16)
    spread = jnp.einsum("ikrje,ikjc->irec", banded, grad_basis, preferred_element_type=jnp.float32)
    summed_ext = (
        jnp.pad(spread[:, 0], ((0, 2), (0, 0), (0, 0)))
        + jnp.pad(spread[:, 1], ((1, 1), (0, 0), (0, 0)))
        + jnp.pad(spread[:, 2], ((2, 0), (0, 0), (0, 0)))
    )
    lat_rims = jnp.stack([summed_ext[0], summed_ext[-1]])
    arrived = extended(lat_rims, (("lat", 0),), 1, False)
    interior = summed_ext[1:-1]
    interior = interior.at[0].add(arrived[0])
    interior = interior.at[-1].add(arrived[3])
    side_rims = jnp.concatenate([interior[:, :HALO], interior[:, lon_cols + HALO :]], axis=1)
    arrived_side = extended(side_rims, (("lon", 1),), HALO, True)
    input_grad = interior[:, HALO : HALO + lon_cols]
    input_grad = input_grad.at[:, :HALO].add(arrived_side[:, :HALO])
    input_grad = input_grad.at[:, lon_cols - HALO :].add(arrived_side[:, 3 * HALO :])
    band_chans = chans // lax.axis_size("lat")
    summed_weight = lax.psum(partial_weight, ("lat", "lon"))
    band_weight = lax.dynamic_slice_in_dim(
        summed_weight, lax.axis_index("lat") * band_chans, band_chans, 1
    )
    weight_grad = band_weight / math.sqrt(nlat_total * nlon_total)
    return (input_grad, weight_grad)


def solution(mesh):
    in_specs = (P("lat", "lon", None), P("lat", "lon", None), P(), P(), P(), P())
    out_specs = (P("lat", "lon", None), P(None, "lat", None))
    return jax.shard_map(shards, mesh=mesh, in_specs=in_specs, out_specs=out_specs, check_vma=False)
```

profile of v0, /device:TPU:1, one launch (start us, length us, event | category | flops | bytes accessed | tf_op | source)
XLA Modules:
  0.0 367.2 jit_solution(3412673658132842354)
XLA Ops:
  7.2 0.0 copy-start
  7.2 0.0 all-reduce.8.cloned.1.call-start
  7.2 2.2 fusion.49
  9.4 3.0 collective-permute-start.4
  12.4 0.2 collective-permute-start.5
  12.7 1.0 pad_dynamic-slice_fusion
  13.7 0.1 slice.164
  13.8 0.1 copy.40
  13.9 1.0 pad_dynamic-slice_fusion.1
  14.9 0.1 slice.166
  15.0 0.1 copy.41
  15.1 0.8 pad_dynamic-slice_fusion.2
  15.9 0.1 broadcast_compare_fusion
  16.0 7.0 %convolution_convert_fusion = bf16[32,9,3,64,128]{4,0,3,2,1:T(8,128)(2,1)} fusion(s32[64,128]{1,0:T(8,128)S(1)} %iota_subtract_fusion, s32[32,3,65]{2,0,1:T(8,128)S(1)} %copy.40, pred[32,65]{1,0:T(8,128)(4,1)S(1)} %slice.165, bf16[32,3,65]{2,0,1:T(8,128)(2,1)S(1)} %copy.41), kind=kOutput, calls=%fused_computation.5 | convolution fusion | flops 927904256 | bytes 14228064 | tf_op jit(solution)/shard_map/ikrd,dje->ikrje/dot_general | solution.py:61
  22.9 0.0 copy-done
  23.0 18.0 %fusion.8 = f32[32,3,128,256]{3,2,1,0:T(8,128)} fusion(bf16[32,9,3,64,128]{4,0,3,2,1:T(8,128)(2,1)} %convolution_convert_fusion, bf16[9,256,256]{2,1,0:T(8,128)(2,1)S(1)} %copy-done, bf16[32,64,256]{2,1,0:T(8,128)(2,1)} %param.15, f32[32]{0:T(128)S(1)} %sine_multiply_fusion), kind=kOutput, calls=%fused_computation.12 | convolution fusion | flops 6046089216 | bytes 28967040 | tf_op jit(solution)/shard_map/ikrje,ikjc->irec/dot_general | solution.py:76
  41.0 9.4 %slice_bitcast_fusion.2 = (f32[32,128,256]{2,1,0:T(8,128)S(1)}, f32[32,128,256]{2,1,0:T(8,128)}, f32[32,128,256]{2,1,0:T(8,128)}) fusion(f32[32,3,128,256]{3,2,1,0:T(8,128)} %fusion.8), kind=kLoop, calls=%fused_computation.15 | loop fusion | bytes 25165824 | tf_op jit(solution)/shard_map/squeeze | solution.py:78
  50.4 0.0 copy-start.2
  50.4 0.0 copy-start.3
  50.4 1.1 pad_add_fusion.1
  51.5 3.2 collective-permute-start
  54.7 1.5 collective-permute-start.1
  56.2 0.0 copy-done.2
  56.2 0.0 copy-done.3
  56.2 3.0 pad_add_fusion
  59.2 2.5 slice.170
  61.7 0.0 copy-start.6
  61.7 0.0 collective-permute-done
  61.8 0.0 collective-permute-done.1
  61.8 0.0 copy-start.4
  61.8 0.0 collective-permute-done.4
  61.8 1.7 constant_dynamic-update-slice_fusion.2
  63.6 0.4 copy-done.6
  64.0 0.1 constant_dynamic-update-slice_fusion.1
  64.1 0.0 collective-permute-done.5
  64.1 1.1 constant_dynamic-update-slice_fusion
  65.2 4.0 %collective-permute-start.6 = (bf16[1,128,256]{2,1,0:T(8,128)(2,1)S(1)}, bf16[1,128,256]{2,1,0:T(8,128)(2,1)S(1)}, u32[]{:S(2)}, u32[]{:S(2)}) collective-permute-start(bf16[1,128,256]{2,1,0:T(8,128)(2,1)S(1)} %get-tuple-element.59), channel_id=1, source_target_pairs={{0,32},{32,64},{64,96},{96,128},{128,160},{160,192},{192,224},{1,3... | collective-permute-start | bytes 196616 | tf_op jit(solution)/shard_map/ppermute | solution.py:19
  69.2 1.3 collective-permute-start.7
  70.5 1.5 fusion.47
  72.0 0.0 copy-done.4
  72.0 2.6 collective-permute-start.2
  74.6 4.0 %collective-permute-start.3 = (f32[32,32,256]{2,1,0:T(8,128)}, f32[32,32,256]{2,1,0:T(8,128)}, u32[]{:S(2)}, u32[]{:S(2)}) collective-permute-start(f32[32,32,256]{2,1,0:T(8,128)} %get-tuple-element.55), channel_id=1, source_target_pairs={{1,0},{2,1},{3,2},{4,3},{5,4},{6,5},{7,6},{8,7},{9,8},{10,9},{11,1... | collective-permute-start | bytes 3145736 | tf_op jit(solution)/shard_map/ppermute | solution.py:22
  78.5 0.0 collective-permute-done.6
  78.5 0.0 collective-permute-done.7
  78.5 2.3 fusion.18
  80.8 13.8 %fusion.19 = f32[9,256,256]{2,1,0:T(8,128)} fusion(bf16[32,9,3,64,128]{4,0,3,2,1:T(8,128)(2,1)} %convolution_convert_fusion, bf16[32,64,256]{2,1,0:T(8,128)(2,1)} %param.15, f32[32]{0:T(128)S(1)} %sine_multiply_fusion, bf16[32,1,128,256]{3,2,0,1:T(8,128)(2,1)} %get-tuple-element.58, bf16[32,1,128,256]{3,2,0,1:T(8,128)(2,1)S(1)} %bitcast.63, ...), kind=kOutput, calls=%fused_computation.24 | convolution fusion | flops 6052380672 | bytes 23855232 | tf_op jit(solution)/shard_map/ikjc,ijo->kco/dot_general | solution.py:70
  94.7 0.0 all-reduce.8.cloned.1.call-update
  94.7 0.0 copy-start.1
  94.7 1.9 slice.172
  96.5 0.0 collective-permute-done.2
  96.6 1.7 fusion.24
  98.3 0.0 collective-permute-done.3
  98.3 1.5 fusion.23
  99.8 0.0 copy-start.5
  99.8 258.9 %all-reduce.8.cloned.1.call-done = f32[9,256,256]{2,1,0:T(8,128)} async-done(((f32[9,256,256]{2,1,0:T(8,128)}), f32[9,256,256]{2,1,0:T(8,128)}) %all-reduce.8.cloned.1.call-update) | async-done | bytes 2359312 | tf_op jit(solution)/shard_map/psum | solution.py:93
  358.7 1.7 dynamic-slice_multiply_fusion
  360.4 0.0 copy-done.5
  360.4 0.0 copy-done.1
  (7 shorter events, 0.1 us)
Async XLA Ops:
  7.2 15.8 %copy-start = (bf16[9,256,256]{2,1,0:T(8,128)(2,1)S(1)}, bf16[9,256,256]{2,1,0:T(8,128)(2,1)}, u32[]{:S(2)}) copy-start(bf16[9,256,256]{2,1,0:T(8,128)(2,1)} %param.16) | copy-start | bytes 3538948
  7.2 351.5 %all-reduce.8.cloned.1.call-start = ((), (), s32[]{:S(2)}) async-start(), calls=%async_computation | async-start | bytes 4718592 | tf_op jit(solution)/shard_map/psum | solution.py:93
  9.4 52.4 %collective-permute-start.4 = (bf16[32,32,256]{2,1,0:T(8,128)(2,1)S(1)}, bf16[32,32,256]{2,1,0:T(8,128)(2,1)}, u32[]{:S(2)}, u32[]{:S(2)}) collective-permute-start(bf16[32,32,256]{2,1,0:T(8,128)(2,1)S(1)} %get-tuple-element.62), channel_id=1, source_target_pairs={{0,1},{1,2},{2,3},{3,4},{4,5},{5,6},{6,7},{7,8},{8,9},{9,10},{10,1... | collective-permute-start | bytes 1572872 | tf_op jit(solution)/shard_map/ppermute | solution.py:19
  12.4 51.7 %collective-permute-start.5 = (bf16[32,32,256]{2,1,0:T(8,128)(2,1)}, bf16[32,32,256]{2,1,0:T(8,128)(2,1)}, u32[]{:S(2)}, u32[]{:S(2)}) collective-permute-start(bf16[32,32,256]{2,1,0:T(8,128)(2,1)} %get-tuple-element.61), channel_id=1, source_target_pairs={{1,0},{2,1},{3,2},{4,3},{5,4},{6,5},{7,6},{8,7},{9,8},{10,9},{11,1... | collective-permute-start | bytes 1572872 | tf_op jit(solution)/shard_map/ppermute | solution.py:22
  50.4 5.7 %copy-start.2 = (f32[32,128,256]{2,1,0:T(8,128)S(1)}, f32[32,128,256]{2,1,0:T(8,128)}, u32[]{:S(2)}) copy-start(f32[32,128,256]{2,1,0:T(8,128)} %get-tuple-element.53) | copy-start | bytes 12582916
  50.4 5.8 %copy-start.3 = (f32[32,128,256]{2,1,0:T(8,128)S(1)}, f32[32,128,256]{2,1,0:T(8,128)}, u32[]{:S(2)}) copy-start(f32[32,128,256]{2,1,0:T(8,128)} %get-tuple-element.54) | copy-start | bytes 12582916
  51.5 10.2 %collective-permute-start = (f32[1,128,256]{2,1,0:T(8,128)S(1)}, f32[1,128,256]{2,1,0:T(8,128)S(1)}, u32[]{:S(2)}, u32[]{:S(2)}) collective-permute-start(f32[1,128,256]{2,1,0:T(8,128)S(1)} %get-tuple-element.51), channel_id=1, source_target_pairs={{0,32},{32,64},{64,96},{96,128},{128,160},{160,192},{192,224},{1,3... | collective-permute-start | bytes 393224 | tf_op jit(solution)/shard_map/ppermute | solution.py:19
  54.7 7.1 %collective-permute-start.1 = (f32[1,128,256]{2,1,0:T(8,128)S(1)}, f32[1,128,256]{2,1,0:T(8,128)S(1)}, u32[]{:S(2)}, u32[]{:S(2)}) collective-permute-start(f32[1,128,256]{2,1,0:T(8,128)S(1)} %get-tuple-element.50), channel_id=1, source_target_pairs={{32,0},{64,32},{96,64},{128,96},{160,128},{192,160},{224,192},{33,... | collective-permute-start | bytes 393224 | tf_op jit(solution)/shard_map/ppermute | solution.py:22
  61.7 2.3 copy-start.6
  61.8 10.2 %copy-start.4 = (f32[32,128,256]{2,1,0:T(8,128)}, f32[32,128,256]{2,1,0:T(8,128)S(1)}, u32[]{:S(2)}) copy-start(f32[32,128,256]{2,1,0:T(8,128)S(1)} %fusion.42) | copy-start | bytes 12582916
  65.2 13.3 %collective-permute-start.6 = (bf16[1,128,256]{2,1,0:T(8,128)(2,1)S(1)}, bf16[1,128,256]{2,1,0:T(8,128)(2,1)S(1)}, u32[]{:S(2)}, u32[]{:S(2)}) collective-permute-start(bf16[1,128,256]{2,1,0:T(8,128)(2,1)S(1)} %get-tuple-element.59), channel_id=1, source_target_pairs={{0,32},{32,64},{64,96},{96,128},{128,160},{160,192},{192,224},{1,3... | collective-permute-start | bytes 196616 | tf_op jit(solution)/shard_map/ppermute | solution.py:19
  69.2 9.3 %collective-permute-start.7 = (bf16[1,128,256]{2,1,0:T(8,128)(2,1)S(1)}, bf16[1,128,256]{2,1,0:T(8,128)(2,1)S(1)}, u32[]{:S(2)}, u32[]{:S(2)}) collective-permute-start(bf16[1,128,256]{2,1,0:T(8,128)(2,1)S(1)} %get-tuple-element.60), channel_id=1, source_target_pairs={{32,0},{64,32},{96,64},{128,96},{160,128},{192,160},{224,192},{33,... | collective-permute-start | bytes 196616 | tf_op jit(solution)/shard_map/ppermute | solution.py:22
  72.0 24.5 %collective-permute-start.2 = (f32[32,32,256]{2,1,0:T(8,128)}, f32[32,32,256]{2,1,0:T(8,128)}, u32[]{:S(2)}, u32[]{:S(2)}) collective-permute-start(f32[32,32,256]{2,1,0:T(8,128)} %get-tuple-element.56), channel_id=1, source_target_pairs={{0,1},{1,2},{2,3},{3,4},{4,5},{5,6},{6,7},{7,8},{8,9},{9,10},{10,1... | collective-permute-start | bytes 3145736 | tf_op jit(solution)/shard_map/ppermute | solution.py:19
  74.6 23.7 %collective-permute-start.3 = (f32[32,32,256]{2,1,0:T(8,128)}, f32[32,32,256]{2,1,0:T(8,128)}, u32[]{:S(2)}, u32[]{:S(2)}) collective-permute-start(f32[32,32,256]{2,1,0:T(8,128)} %get-tuple-element.55), channel_id=1, source_target_pairs={{1,0},{2,1},{3,2},{4,3},{5,4},{6,5},{7,6},{8,7},{9,8},{10,9},{11,1... | collective-permute-start | bytes 3145736 | tf_op jit(solution)/shard_map/ppermute | solution.py:22
  94.7 265.7 %copy-start.1 = (bf16[9,256,256]{2,1,0:T(8,128)(2,1)S(1)}, bf16[9,256,256]{2,1,0:T(8,128)(2,1)}, u32[]{:S(2)}) copy-start(bf16[9,256,256]{2,1,0:T(8,128)(2,1)} %param.16) | copy-start | bytes 3538948
  99.8 260.6 %copy-start.5 = (f32[32,64,256]{2,1,0:T(8,128)}, f32[32,64,256]{2,1,0:T(8,128)S(1)}, u32[]{:S(2)}) copy-start(f32[32,64,256]{2,1,0:T(8,128)S(1)} %fusion.23) | copy-start | bytes 6291460
Sparse Core Ops, SparseCore 0:
  94.8 263.8 all-reduce.7
where the time goes:
time: 368 us; the launch traced here: 367 us
  waiting for transfers between devices  259 us (70%)
  matrix products  38.9 us (11%)
  local copies, waits for them, and re-layouts  24 us (7%)
  starting transfers between devices  19.7 us (5%)
  between operations  14.3 us (4%)
  other arithmetic  11.5 us (3%)
    psum x1, waiting for transfers between devices, shards(): summed_weight = lax.psum(partial_weight, ('lat', 'lon'))  259 us
    dot_general x1, matrix products, shards(): jnp.einsum('ikrje,ikjc->irec', banded, grad_basis, preferred_element_type...  18 us
    dot_general x1, matrix products, shards(): jnp.einsum('ikjc,ijo->kco', basis_out, out_grad, preferred_element_type=j...  13.8 us
    ppermute x4, starting transfers between devices, extended(): lax.ppermute(lax.slice_in_dim(block, block.shape[dim] - width, None, axis...  12.7 us
    squeeze x1, local copies, waits for them, and re-layouts, shards(): spread[:, 0]  9.44 us
  transfers between devices with their start and end apart: 9, of which 1 were waited for; matrix products, arithmetic and copies ran while one was open for 19% of the time, Pallas kernels for 0%

commit v1 on v0

v1 whole, which is shorter than its diff:
```python
import functools
import math

import jax
import jax.numpy as jnp
import numpy as np
from jax import lax
from jax.experimental import pallas as pl
from jax.experimental.pallas import tpu as pltpu
from jax.sharding import PartitionSpec as P

K = 9
HALO = 32
GROUP = 3
GROUPS = K // GROUP
WINDOW = 16
REACH = WINDOW + 2 * HALO
DEPTH = 3 * REACH
MESH = pl.DeviceIdType.MESH
BF16 = jnp.bfloat16
F32 = jnp.float32


def dot(a, b, dims):
    return lax.dot_general(a, b, (dims, ((), ())), preferred_element_type=F32)


def kernel(
    sizes,
    cot_hbm, field_hbm, weight_hbm, values_hbm, index_hbm, width_hbm, area_ref,
    grad_ref, wgrad_ref,
    cot, field, weight, values, index, width, flip_v, flip_i, taps, spread,
    part, pair, half, lat_in, band, lon_in, final,
    load_sems, halo_send, halo_recv, pair_send, pair_recv, lat_send, lat_recv,
    lon_send, lon_recv, all_send, all_recv, mate_send, mate_recv,
):
    n_lat, n_lon, rows, cols, chans, nlat, scale = sizes
    side_cols = cols // 2
    side_spots = rows * side_cols
    chips = n_lon // 2
    wide = chans // n_lat
    lanes = chans // 2
    lat = lax.axis_index("lat")
    lon = lax.axis_index("lon")
    core = lax.rem(lon, 2)
    chip = lax.div(lon, 2)
    has_up = lat > 0
    has_down = lat < n_lat - 1
    west = lax.rem(lon + n_lon - 1, n_lon)
    east = lax.rem(lon + 1, n_lon)
    mate = lon + 1 - 2 * core

    loads = [
        pltpu.make_async_copy(values_hbm, values, load_sems.at[0]),
        pltpu.make_async_copy(index_hbm, index, load_sems.at[1]),
        pltpu.make_async_copy(width_hbm, width, load_sems.at[2]),
        pltpu.make_async_copy(
            cot_hbm, cot.at[pl.ds(1, rows), pl.ds(HALO, cols)], load_sems.at[3]
        ),
        pltpu.make_async_copy(
            field_hbm.at[:, pl.ds(0, side_cols)], field.at[0], load_sems.at[4]
        ),
        pltpu.make_async_copy(
            field_hbm.at[:, pl.ds(side_cols, side_cols)], field.at[1], load_sems.at[5]
        ),
        pltpu.make_async_copy(weight_hbm, weight, load_sems.at[6]),
    ]
    for load in loads:
        load.start()

    barrier = pltpu.get_barrier_semaphore()

    def greet(device):
        pl.semaphore_signal(barrier, inc=1, device_id=device, device_id_type=MESH)

    def greet_corner(target):
        greet((target, west))
        greet((target, east))

    greet((lat, west))
    greet((lat, east))
    pl.when(has_up)(lambda: greet_corner(lat - 1))
    pl.when(has_down)(lambda: greet_corner(lat + 1))

    @pl.loop(1, n_lat)
    def _(step):
        greet((lax.rem(lat + step, n_lat), lon))

    @pl.loop(1, chips)
    def _(step):
        greet((lat, lax.rem(lon + 2 * step, n_lon)))

    corners = 2 * (has_up.astype(jnp.int32) + has_down.astype(jnp.int32))
    pl.semaphore_wait(barrier, n_lat - 1 + chips - 1 + 2 + corners)

    def halo(slot, source, target, device):
        return pltpu.make_async_remote_copy(
            src_ref=source, dst_ref=target,
            send_sem=halo_send.at[slot], recv_sem=halo_recv.at[slot],
            device_id=device, device_id_type=MESH,
        )

    low = pl.ds(0, HALO)
    high = pl.ds(cols - HALO, HALO)
    ext_low = pl.ds(0, HALO)
    ext_mid = pl.ds(HALO, cols)
    ext_high = pl.ds(cols + HALO, HALO)
    own_rows = pl.ds(1, rows)
    first, last = pl.ds(0, 1), pl.ds(rows - 1, 1)
    above, below = pl.ds(0, 1), pl.ds(rows + 1, 1)
    to_east = halo(0, cot_hbm.at[:, high], cot.at[own_rows, ext_low], (lat, east))
    to_west = halo(1, cot_hbm.at[:, low], cot.at[own_rows, ext_high], (lat, west))
    down = [
        halo(2, cot_hbm.at[last, high], cot.at[above, ext_low], (lat + 1, east)),
        halo(3, cot_hbm.at[last, low], cot.at[above, ext_high], (lat + 1, west)),
        halo(4, cot_hbm.at[last], cot.at[above, ext_mid], (lat + 1, lon)),
    ]
    up = [
        halo(5, cot_hbm.at[first, high], cot.at[below, ext_low], (lat - 1, east)),
        halo(6, cot_hbm.at[first, low], cot.at[below, ext_high], (lat - 1, west)),
        halo(7, cot_hbm.at[first], cot.at[below, ext_mid], (lat - 1, lon)),
    ]

    @pl.when(has_down)
    def _():
        for copy in down:
            copy.start()

    @pl.when(has_up)
    def _():
        for copy in up:
            copy.start()

    to_east.start()
    to_west.start()

    for load in loads[:3]:
        load.wait()
    size = 2 * HALO + 1
    tap_in = lax.broadcasted_iota(jnp.int32, (size, 128), 0)
    tap_out = lax.broadcasted_iota(jnp.int32, (size, 128), 1)
    reverse = jnp.where(tap_in + tap_out == 2 * HALO, 1.0, 0.0).astype(BF16)
    offset = jnp.abs(lax.broadcasted_iota(jnp.int32, (size, nlat), 0) - HALO)
    inside = offset <= width[...]
    for r in range(3):
        which = jnp.where(inside, index[r], K).astype(F32).astype(BF16)
        flip_v[r] = dot(values[r], reverse, ((0,), (0,)))
        flip_i[r] = dot(which, reverse, ((0,), (0,)))

    def clip_row(row):
        return jnp.clip(lat * rows + row - 1, 0, nlat - 1)

    @pl.loop(0, rows, unroll=8)
    def _(row):
        vals = jnp.zeros((WINDOW, 256), F32)
        which = jnp.zeros((WINDOW, 256), F32)
        rest = jnp.zeros((WINDOW, 128), F32)
        for t in range(3):
            at = pl.ds(clip_row(row + t), 1)
            spots = [
                jnp.concatenate(
                    [jnp.broadcast_to(table[2 - t, at, :], (WINDOW, 128)), rest], axis=1
                )
                for table in (flip_v, flip_i)
            ]
            spots = [pltpu.roll(x, REACH * t, 1, stride=1, stride_axis=0) for x in spots]
            vals += spots[0]
            which += spots[1]
        vals = vals.astype(BF16)
        which = which.astype(BF16)
        for k in range(K):
            taps[row, k * WINDOW : (k + 1) * WINDOW] = jnp.where(
                which == BF16(k), vals, jnp.zeros_like(vals)
            )

    def scale_rows(at, start, stop, columns):
        def body(row):
            factor = area_ref[clip_row(row)]
            cot[row, at] = (cot[row, at].astype(F32) * factor).astype(BF16)

        pl.loop(start, stop, unroll=4)(body)

    loads[3].wait()
    scale_rows(ext_mid, 1, rows + 1, cols)

    @pl.when(has_up)
    def _():
        for copy in down:
            copy.wait_recv()

    @pl.when(has_down)
    def _():
        for copy in up:
            copy.wait_recv()

    @pl.when(jnp.logical_not(has_up))
    def _():
        cot[0] = jnp.zeros_like(cot[0])

    @pl.when(jnp.logical_not(has_down))
    def _():
        cot[rows + 1] = jnp.zeros_like(cot[rows + 1])

    for edge in (0, rows + 1):
        cot[edge] = (cot[edge].astype(F32) * area_ref[clip_row(edge)]).astype(BF16)

    def filter_side(side):
        at = pl.ds(pl.multiple_of(side * (HALO + cols), HALO), HALO)

        def scale_row(row):
            factor = area_ref[clip_row(row)]
            cot[row, at] = (cot[row, at].astype(F32) * factor).astype(BF16)

        pl.loop(1, rows + 1, unroll=4)(scale_row)

        def filter_row(row):
            lhs = taps[row][:, :DEPTH]
            for u in range(side_cols // WINDOW):
                start = pl.multiple_of(side * side_cols + u * WINDOW, WINDOW)
                rhs = cot[pl.ds(row, 3), pl.ds(start, REACH)].reshape(DEPTH, chans)
                result = dot(lhs, rhs, ((1,), (0,))).astype(BF16)
                to = pl.ds(pl.multiple_of(row * side_cols + u * WINDOW, WINDOW), WINDOW)
                for k in range(K):
                    spread[side, k, to] = result[k * WINDOW : (k + 1) * WINDOW]

        pl.loop(0, rows, unroll=16)(filter_row)

    def field_product(side, k):
        lhs = field[side].reshape(side_spots, chans)
        return dot(lhs, spread[side, k], ((0,), (0,)))

    near = 1 - core
    far = core

    @pl.when(core == 0)
    def _():
        to_west.wait_recv()

    @pl.when(core == 1)
    def _():
        to_east.wait_recv()

    filter_side(near)
    loads[4].wait()
    loads[5].wait()
    for k in range(K):
        result = field_product(near, k)
        part[0, k] = result[:, :lanes]
        part[1, k] = result[:, lanes:]

    @pl.when(core == 0)
    def _():
        to_east.wait_recv()

    @pl.when(core == 1)
    def _():
        to_west.wait_recv()

    filter_side(far)

    def pair_copy(group):
        ks = pl.ds(group * GROUP, GROUP)
        return pltpu.make_async_remote_copy(
            src_ref=part.at[1 - core, ks], dst_ref=pair.at[ks],
            send_sem=pair_send.at[group], recv_sem=pair_recv.at[group],
            device_id=(lat, mate), device_id_type=MESH,
        )

    def lat_copy(group, step):
        ks = pl.ds(group * GROUP, GROUP)
        peer = lax.rem(lat + step, n_lat)
        return pltpu.make_async_remote_copy(
            src_ref=half.at[ks, pl.ds(pl.multiple_of(peer * wide, wide), wide)],
            dst_ref=lat_in.at[step, ks],
            send_sem=lat_send.at[group, step], recv_sem=lat_recv.at[group, step],
            device_id=(peer, lon), device_id_type=MESH,
        )

    def owner_of(k):
        return (k * chips) // K

    def lon_copy(k, step):
        return pltpu.make_async_remote_copy(
            src_ref=band.at[k], dst_ref=lon_in.at[step],
            send_sem=lon_send.at[k], recv_sem=lon_recv.at[step],
            device_id=(lat, owner_of(k) * 2 + core), device_id_type=MESH,
        )

    def reduce_pair(group):
        pair_copy(group).wait_recv()
        for k in range(group * GROUP, (group + 1) * GROUP):
            half[k] = (part[core, k] + pair[k]).astype(BF16)

        @pl.loop(1, n_lat)
        def _(step):
            lat_copy(group, step).start()

    def reduce_lat(group):
        @pl.loop(1, n_lat)
        def _(step):
            lat_copy(group, step).wait_recv()

        at = pl.ds(pl.multiple_of(lat * wide, wide), wide)
        for k in range(group * GROUP, (group + 1) * GROUP):
            total = half[k, at].astype(F32)
            for step in range(1, n_lat):
                total += lat_in[step, k].astype(F32)
            band[k] = total

            @pl.when(chip != owner_of(k))
            def _():
                lon_copy(k, lax.rem(owner_of(k) - chip + chips, chips)).start()

    for group in range(GROUPS):
        for k in range(group * GROUP, (group + 1) * GROUP):
            result = field_product(far, k)
            part[0, k] += result[:, :lanes]
            part[1, k] += result[:, lanes:]
        pair_copy(group).start()
        if group > 0:
            reduce_pair(group - 1)

    loads[6].wait()

    def grad_block(side, block):
        at = pl.ds(block * 256, 256)
        total = dot(spread[side, 0, at], weight[0], ((1,), (1,)))
        for k in range(1, K):
            total += dot(spread[side, k, at], weight[k], ((1,), (1,)))
        tall = 256 // side_cols
        to = pl.ds(block * tall, tall)
        grad_ref[to, side * side_cols : (side + 1) * side_cols] = total.reshape(
            tall, side_cols, chans
        )

    blocks = [(side, block) for side in range(2) for block in range(side_spots // 256)]
    share = -(-len(blocks) // 4)
    for block in blocks[:share]:
        grad_block(*block)
    reduce_pair(GROUPS - 1)
    for block in blocks[share : 2 * share]:
        grad_block(*block)
    reduce_lat(0)
    for block in blocks[2 * share : 3 * share]:
        grad_block(*block)
    reduce_lat(1)
    for block in blocks[3 * share :]:
        grad_block(*block)
    reduce_lat(2)

    def all_copy(k, step):
        return pltpu.make_async_remote_copy(
            src_ref=final.at[core, k], dst_ref=final.at[core, k],
            send_sem=all_send.at[step], recv_sem=all_recv.at[k],
            device_id=(lat, lax.rem(lon + 2 * step, n_lon)), device_id_type=MESH,
        )

    def mate_copy(k):
        return pltpu.make_async_remote_copy(
            src_ref=final.at[core, k], dst_ref=final.at[core, k],
            send_sem=mate_send.at[k], recv_sem=mate_recv.at[k],
            device_id=(lat, mate), device_id_type=MESH,
        )

    for k in range(K):
        @pl.when(chip == owner_of(k))
        def _():
            @pl.loop(1, chips)
            def _(step):
                lon_copy(k, step).wait_recv()

            total = band[k]
            for step in range(1, chips):
                total += lon_in[step]
            final[core, k] = (total * scale).astype(BF16)

            @pl.loop(1, chips)
            def _(step):
                all_copy(k, step).start()

            mate_copy(k).start()

    for k in range(K):
        @pl.when(chip != owner_of(k))
        def _():
            all_copy(k, 0).wait_recv()
            mate_copy(k).start()

    for k in range(K):
        mate_copy(k).wait_recv()
        for side in range(2):
            wgrad_ref[k, :, side * lanes : (side + 1) * lanes] = final[side, k].astype(F32)

    to_east.wait_send()
    to_west.wait_send()

    @pl.when(has_down)
    def _():
        for copy in down:
            copy.wait_send()

    @pl.when(has_up)
    def _():
        for copy in up:
            copy.wait_send()

    for group in range(GROUPS):
        pair_copy(group).wait_send()

        @pl.loop(1, n_lat)
        def _(step):
            lat_copy(group, step).wait_send()

    for k in range(K):
        mate_copy(k).wait_send()

        @pl.when(chip != owner_of(k))
        def _():
            lon_copy(k, 0).wait_send()

        @pl.when(chip == owner_of(k))
        def _():
            @pl.loop(1, chips)
            def _(step):
                all_copy(k, step).wait_send()


def shards(input_field, cotangent, weight, basis_values, basis_index, halo_width):
    n_lat = lax.axis_size("lat")
    n_lon = lax.axis_size("lon")
    rows, cols, chans = input_field.shape
    nlat = rows * n_lat
    chips = n_lon // 2
    wide = chans // n_lat
    lanes = chans // 2
    side_cols = cols // 2
    ext = cols + 2 * HALO
    size = 2 * HALO + 1
    centres = np.arange(nlat, dtype=np.float32) + np.float32(0.5)
    area = np.float32(np.pi / 2) * np.sin(np.float32(np.pi) * centres / np.float32(nlat))
    scale = 1.0 / math.sqrt(nlat * cols * n_lon)
    sizes = (n_lat, n_lon, rows, cols, chans, nlat, scale)
    whole = pl.BlockSpec(memory_space=pltpu.HBM)
    vmem = pl.BlockSpec(memory_space=pltpu.VMEM)
    smem = pl.BlockSpec(memory_space=pltpu.SMEM)
    dma = pltpu.SemaphoreType.DMA
    table = pltpu.VMEM((3, nlat, 128), F32)
    return pl.pallas_call(
        functools.partial(kernel, sizes),
        out_shape=(
            pltpu.VMEM((rows, cols, chans), F32),
            pltpu.VMEM((K, wide, chans), F32),
        ),
        in_specs=[whole] * 6 + [smem],
        out_specs=(vmem, vmem),
        scratch_shapes=[
            pltpu.VMEM((rows + 2, ext, chans), BF16),
            pltpu.VMEM((2, rows, side_cols, chans), BF16),
            pltpu.VMEM((K, chans, chans), BF16),
            pltpu.VMEM((3, size, nlat), BF16),
            pltpu.VMEM((3, size, nlat), jnp.int32),
            pltpu.VMEM((1, nlat), jnp.int32),
            table, table,
            pltpu.VMEM((rows, K * WINDOW, 256), BF16),
            pltpu.VMEM((2, K, rows * side_cols, chans), BF16),
            pltpu.VMEM((2, K, chans, lanes), F32),
            pltpu.VMEM((K, chans, lanes), F32),
            pltpu.VMEM((K, chans, lanes), BF16),
            pltpu.VMEM((n_lat, K, wide, lanes), BF16),
            pltpu.VMEM((K, wide, lanes), F32),
            pltpu.VMEM((chips, wide, lanes), F32),
            pltpu.VMEM((2, K, wide, lanes), BF16),
            dma((7,)), dma((8,)), dma((8,)), dma((GROUPS,)), dma((GROUPS,)),
            dma((GROUPS, n_lat)), dma((GROUPS, n_lat)), dma((K,)), dma((chips,)),
            dma((chips,)), dma((K,)), dma((K,)), dma((K,)),
        ],
        compiler_params=pltpu.CompilerParams(
            collective_id=0, has_side_effects=True, vmem_limit_bytes=40 * 2**20
        ),
        cost_estimate=pl.CostEstimate(
            flops=2 * K * rows * cols * chans * (3 * ext + 2 * chans),
            bytes_accessed=6 * 2**20, transcendentals=0,
        ),
    )(
        cotangent, input_field, weight,
        basis_values.transpose(1, 2, 0), basis_index.transpose(1, 2, 0),
        halo_width.reshape(1, nlat), jnp.asarray(area),
    )


def solution(mesh):
    in_specs = (P("lat", "lon", None), P("lat", "lon", None), P(), P(), P(), P())
    out_specs = (P("lat", "lon", None), P(None, "lat", None))
    return jax.shard_map(shards, mesh=mesh, in_specs=in_specs, out_specs=out_specs, check_vma=False)
```

time: 368 us -> 67.1 us (0.18)
  waiting for transfers between devices: 259 us -> 0 us
  Pallas kernels: 0 us -> 57.2 us
  matrix products: 38.9 us -> 0 us
  starting transfers between devices: 19.7 us -> 0 us
  local copies, waits for them, and re-layouts: 24 us -> 8.94 us
  between operations: 14.3 us -> 0.65 us
  other arithmetic: 11.5 us -> 0 us
    psum x1 -> x0, waiting for transfers between devices: 259 us -> none  [shards(): summed_weight = lax.psum(partial_weight, ('lat', 'lon'))]
    pallas_call x0 -> x1, Pallas kernels: none -> 57.2 us  [shards(): pl.pallas_call(functools.partial(kernel, sizes), out_shape=(pltpu.VMEM((r...]
    dot_general x3 -> x0, matrix products: 38.9 us -> none  [the longest x1 18 us: shards(): jnp.einsum('ikrje,ikjc->irec', banded, grad_basis, preferred_element_type...]
    ppermute x8 -> x0, starting transfers between devices: 19.7 us -> none  [the longest x4 12.7 us: extended(): lax.ppermute(lax.slice_in_dim(block, block.shape[dim] - width, None, axis...]
    squeeze x1 -> x0, local copies, waits for them, and re-layouts: 9.44 us -> none  [shards(): spread[:, 0]]
    slice x8 -> x0, local copies, waits for them, and re-layouts: 8.18 us -> none  [the longest x1 2.46 us: shards(): interior = summed_ext[1:-1]]
    unnamed x18 -> x16, local copies, waits for them, and re-layouts: 2.46 us -> 8.94 us
  transfers between devices with their start and end apart: 9 -> 0, of which waited for: 1 -> 0; matrix products, arithmetic and copies ran while one was open for 19% -> 0% of each run, Pallas kernels for 0% -> 0%
where the time goes in v1:
time: 67.1 us; the launch traced here: 66.8 us
  Pallas kernels  57.2 us (85%)
  local copies, waits for them, and re-layouts  8.94 us (13%)
    pallas_call x1, Pallas kernels, shards(): pl.pallas_call(functools.partial(kernel, sizes), out_shape=(pltpu.VMEM((r...  57.2 us
    unnamed x16, local copies, waits for them, and re-layouts  8.94 us

profile of v1, /device:TPU:1, one launch (start us, length us, event | category | flops | bytes accessed | tf_op | source)
XLA Modules:
  0.0 66.8 jit_solution(16037282700188045436)
XLA Ops:
  0.6 0.0 copy-start
  0.6 1.3 %copy-done = bf16[9,256,256]{2,1,0:T(8,128)(2,1)S(1)} copy-done((bf16[9,256,256]{2,1,0:T(8,128)(2,1)S(1)}, bf16[9,256,256]{2,1,0:T(8,128)(2,1)}, u32[]{:S(2)}) %copy-start) | copy-done | bytes 1179672
  1.9 0.0 copy-start.1
  1.9 1.2 %copy-done.1 = bf16[32,64,256]{2,1,0:T(8,128)(2,1)S(1)} copy-done((bf16[32,64,256]{2,1,0:T(8,128)(2,1)S(1)}, bf16[32,64,256]{2,1,0:T(8,128)(2,1)}, u32[]{:S(2)}) %copy-start.1) | copy-done | bytes 1048600
  3.1 0.0 copy-start.2
  3.1 1.2 %copy-done.2 = bf16[32,64,256]{2,1,0:T(8,128)(2,1)S(1)} copy-done((bf16[32,64,256]{2,1,0:T(8,128)(2,1)S(1)}, bf16[32,64,256]{2,1,0:T(8,128)(2,1)}, u32[]{:S(2)}) %copy-start.2) | copy-done | bytes 1048600
  4.4 0.0 copy-start.3
  4.4 0.9 %copy-done.3 = s32[256,3,65]{0,2,1:T(8,128)S(1)} copy-done((s32[256,3,65]{0,2,1:T(8,128)S(1)}, s32[256,3,65]{0,2,1:T(8,128)}, u32[]{:S(2)}) %copy-start.3) | copy-done | bytes 199704
  5.3 0.0 copy-start.4
  5.3 0.9 %copy-done.4 = bf16[256,3,65]{0,2,1:T(8,128)(2,1)S(1)} copy-done((bf16[256,3,65]{0,2,1:T(8,128)(2,1)S(1)}, bf16[256,3,65]{0,2,1:T(8,128)(2,1)}, u32[]{:S(2)}) %copy-start.4) | copy-done | bytes 99864
  6.2 0.0 copy-start.5
  6.2 0.7 %copy-done.5 = s32[256]{0:T(256)S(1)} copy-done((s32[256]{0:T(256)S(1)}, s32[256]{0:T(256)}, u32[]{:S(2)}) %copy-start.5) | copy-done | bytes 1048
  6.9 0.0 copy-start.6
  6.9 0.7 %copy-done.6 = f32[256]{0:T(256)S(1)} copy-done((f32[256]{0:T(256)S(1)}, f32[256]{0:T(256)}, u32[]{:S(2)}) %copy-start.6) | copy-done | bytes 1048
  7.5 57.2 %shard_map.86 = (f32[32,64,256]{2,1,0:T(8,128)S(1)}, f32[9,32,256]{2,1,0:T(8,128)S(1)}) custom-call(bf16[32,64,256]{2,1,0:T(8,128)(2,1)S(1)} %copy-done.1, bf16[32,64,256]{2,1,0:T(8,128)(2,1)S(1)} %copy-done.2, bf16[9,256,256]{2,1,0:T(8,128)(2,1)S(1)} %copy-done, bf16[3,65,256]{2,1,0:T(8,128)(2,1)S(1)} %bitcast.4, s32[3,65,256]{2,1,0:T(8,128)S(1)} %bitcast.3, ...), custom_call_target="tpu_custom_call" | custom-call | flops 8455716864 | bytes 6291456 | tf_op jit(solution)/shard_map/pallas_call | solution.py:448
  64.8 1.3 %copy.11 = f32[32,64,256]{2,1,0:T(8,128)} copy(f32[32,64,256]{2,1,0:T(8,128)S(1)} %get-tuple-element.2) | data formatting | bytes 4194304
  66.1 0.7 %copy.12 = f32[9,32,256]{2,1,0:T(8,128)} copy(f32[9,32,256]{2,1,0:T(8,128)S(1)} %get-tuple-element.3) | data formatting | bytes 589824
Async XLA Ops:
  0.6 1.3 %copy-start = (bf16[9,256,256]{2,1,0:T(8,128)(2,1)S(1)}, bf16[9,256,256]{2,1,0:T(8,128)(2,1)}, u32[]{:S(2)}) copy-start(bf16[9,256,256]{2,1,0:T(8,128)(2,1)} %weight_hbm.1) | copy-start | bytes 3538948
  1.9 1.2 %copy-start.1 = (bf16[32,64,256]{2,1,0:T(8,128)(2,1)S(1)}, bf16[32,64,256]{2,1,0:T(8,128)(2,1)}, u32[]{:S(2)}) copy-start(bf16[32,64,256]{2,1,0:T(8,128)(2,1)} %cot_hbm.1) | copy-start | bytes 3145732
  3.1 1.2 %copy-start.2 = (bf16[32,64,256]{2,1,0:T(8,128)(2,1)S(1)}, bf16[32,64,256]{2,1,0:T(8,128)(2,1)}, u32[]{:S(2)}) copy-start(bf16[32,64,256]{2,1,0:T(8,128)(2,1)} %field_hbm.1) | copy-start | bytes 3145732
  4.4 0.9 %copy-start.3 = (s32[256,3,65]{0,2,1:T(8,128)S(1)}, s32[256,3,65]{0,2,1:T(8,128)}, u32[]{:S(2)}) copy-start(s32[256,3,65]{0,2,1:T(8,128)} %param.11) | copy-start | bytes 599044
  5.3 0.9 %copy-start.4 = (bf16[256,3,65]{0,2,1:T(8,128)(2,1)S(1)}, bf16[256,3,65]{0,2,1:T(8,128)(2,1)}, u32[]{:S(2)}) copy-start(bf16[256,3,65]{0,2,1:T(8,128)(2,1)} %param.10) | copy-start | bytes 299524
  6.2 0.7 %copy-start.5 = (s32[256]{0:T(256)S(1)}, s32[256]{0:T(256)}, u32[]{:S(2)}) copy-start(s32[256]{0:T(256)} %param.12) | copy-start | bytes 3076
  6.9 0.7 %copy-start.6 = (f32[256]{0:T(256)S(1)}, f32[256]{0:T(256)}, u32[]{:S(2)}) copy-start(f32[256]{0:T(256)} %constant.2.clone.area_ref) | copy-start | bytes 3076

commit v2 on v1

--- a/solution.py
+++ b/solution.py
@@ -3,7 +3,6 @@
 
 import jax
 import jax.numpy as jnp
-import numpy as np
 from jax import lax
 from jax.experimental import pallas as pl
 from jax.experimental.pallas import tpu as pltpu
@@ -14,6 +13,7 @@
 GROUP = 3
 GROUPS = K // GROUP
 WINDOW = 16
+CHUNKS = 4
 REACH = WINDOW + 2 * HALO
 DEPTH = 3 * REACH
 MESH = pl.DeviceIdType.MESH
@@ -27,9 +27,9 @@
 
 def kernel(
     sizes,
-    cot_hbm, field_hbm, weight_hbm, values_hbm, index_hbm, width_hbm, area_ref,
+    cot_hbm, field_hbm, weight_hbm, values_hbm, index_hbm, width_hbm,
     grad_ref, wgrad_ref,
-    cot, field, weight, values, index, width, flip_v, flip_i, taps, spread,
+    cot, field, weight, values, index, width, flip_v, flip_i, area, taps, spread,
     part, pair, half, lat_in, band, lon_in, final,
     load_sems, halo_send, halo_recv, pair_send, pair_recv, lat_send, lat_recv,
     lon_send, lon_recv, all_send, all_recv, mate_send, mate_recv,
@@ -100,26 +100,51 @@
             device_id=device, device_id_type=MESH,
         )
 
+    near = 1 - core
+    far = core
+    far_lon = lax.rem(lon + n_lon - 1 + 2 * core, n_lon)
+    tall = rows // CHUNKS
+
+    def columns(start, count):
+        return pl.ds(pl.multiple_of(start, HALO), count)
+
+    def far_copy(chunk, inward):
+        side = far if inward else 1 - far
+        return halo(
+            chunk,
+            cot_hbm.at[pl.ds(chunk * tall, tall), columns(core * (cols - HALO), HALO)],
+            cot.at[pl.ds(1 + chunk * tall, tall), columns(side * (cols + HALO), HALO)],
+            (lat, far_lon),
+        )
+
+    def near_copy(inward):
+        side = near if inward else 1 - near
+        return halo(
+            CHUNKS,
+            cot_hbm.at[:, columns((1 - core) * (cols - HALO), HALO)],
+            cot.at[pl.ds(1, rows), columns(side * (cols + HALO), HALO)],
+            (lat, mate),
+        )
+
     low = pl.ds(0, HALO)
     high = pl.ds(cols - HALO, HALO)
     ext_low = pl.ds(0, HALO)
     ext_mid = pl.ds(HALO, cols)
     ext_high = pl.ds(cols + HALO, HALO)
-    own_rows = pl.ds(1, rows)
     first, last = pl.ds(0, 1), pl.ds(rows - 1, 1)
     above, below = pl.ds(0, 1), pl.ds(rows + 1, 1)
-    to_east = halo(0, cot_hbm.at[:, high], cot.at[own_rows, ext_low], (lat, east))
-    to_west = halo(1, cot_hbm.at[:, low], cot.at[own_rows, ext_high], (lat, west))
     down = [
-        halo(2, cot_hbm.at[last, high], cot.at[above, ext_low], (lat + 1, east)),
-        halo(3, cot_hbm.at[last, low], cot.at[above, ext_high], (lat + 1, west)),
-        halo(4, cot_hbm.at[last], cot.at[above, ext_mid], (lat + 1, lon)),
+        halo(5, cot_hbm.at[last, high], cot.at[above, ext_low], (lat + 1, east)),
+        halo(6, cot_hbm.at[last, low], cot.at[above, ext_high], (lat + 1, west)),
+        halo(7, cot_hbm.at[last], cot.at[above, ext_mid], (lat + 1, lon)),
     ]
     up = [
-        halo(5, cot_hbm.at[first, high], cot.at[below, ext_low], (lat - 1, east)),
-        halo(6, cot_hbm.at[first, low], cot.at[below, ext_high], (lat - 1, west)),
-        halo(7, cot_hbm.at[first], cot.at[below, ext_mid], (lat - 1, lon)),
+        halo(8, cot_hbm.at[first, high], cot.at[below, ext_low], (lat - 1, east)),
+        halo(9, cot_hbm.at[first, low], cot.at[below, ext_high], (lat - 1, west)),
+        halo(10, cot_hbm.at[first], cot.at[below, ext_mid], (lat - 1, lon)),
     ]
+    far_copy(0, False).start()
+    near_copy(False).start()
 
     @pl.when(has_down)
     def _():
@@ -131,8 +156,11 @@
         for copy in up:
             copy.start()
 
-    to_east.start()
-    to_west.start()
+    for chunk in range(1, CHUNKS):
+        far_copy(chunk, False).start()
+
+    latitude = lax.broadcasted_iota(jnp.int32, area.shape, 0) + (lat * rows - 1)
+    area[...] = (math.pi / 2) * jnp.sin(math.pi * (latitude.astype(F32) + 0.5) / nlat)
 
     for load in loads[:3]:
         load.wait()
@@ -173,15 +201,16 @@
                 which == BF16(k), vals, jnp.zeros_like(vals)
             )
 
-    def scale_rows(at, start, stop, columns):
-        def body(row):
-            factor = area_ref[clip_row(row)]
-            cot[row, at] = (cot[row, at].astype(F32) * factor).astype(BF16)
-
-        pl.loop(start, stop, unroll=4)(body)
+    def scale_row(row, at):
+        factor = area[pl.ds(row, 1), :]
+        factor = jnp.concatenate([factor] * (chans // 128), axis=1)
+        cot[row, at] = (cot[row, at].astype(F32) * factor).astype(BF16)
+
+    def scale_edge(row):
+        scale_row(row, pl.ds(0, cols + 2 * HALO))
 
     loads[3].wait()
-    scale_rows(ext_mid, 1, rows + 1, cols)
+    pl.loop(1, rows + 1, unroll=4)(lambda row: scale_row(row, ext_mid))
 
     @pl.when(has_up)
     def _():
@@ -201,62 +230,52 @@
     def _():
         cot[rows + 1] = jnp.zeros_like(cot[rows + 1])
 
-    for edge in (0, rows + 1):
-        cot[edge] = (cot[edge].astype(F32) * area_ref[clip_row(edge)]).astype(BF16)
-
-    def filter_side(side):
-        at = pl.ds(pl.multiple_of(side * (HALO + cols), HALO), HALO)
-
-        def scale_row(row):
-            factor = area_ref[clip_row(row)]
-            cot[row, at] = (cot[row, at].astype(F32) * factor).astype(BF16)
-
-        pl.loop(1, rows + 1, unroll=4)(scale_row)
-
-        def filter_row(row):
+    scale_edge(0)
+    scale_edge(rows + 1)
+
+    def filter_rows(side, start, stop):
+        for row in range(start, stop):
             lhs = taps[row][:, :DEPTH]
             for u in range(side_cols // WINDOW):
-                start = pl.multiple_of(side * side_cols + u * WINDOW, WINDOW)
-                rhs = cot[pl.ds(row, 3), pl.ds(start, REACH)].reshape(DEPTH, chans)
+                at = pl.ds(pl.multiple_of(side * side_cols + u * WINDOW, WINDOW), REACH)
+                rhs = cot[row : row + 3, at].reshape(DEPTH, chans)
                 result = dot(lhs, rhs, ((1,), (0,))).astype(BF16)
-                to = pl.ds(pl.multiple_of(row * side_cols + u * WINDOW, WINDOW), WINDOW)
+                to = row * side_cols + u * WINDOW
                 for k in range(K):
-                    spread[side, k, to] = result[k * WINDOW : (k + 1) * WINDOW]
-
-        pl.loop(0, rows, unroll=16)(filter_row)
-
-    def field_product(side, k):
-        lhs = field[side].reshape(side_spots, chans)
-        return dot(lhs, spread[side, k], ((0,), (0,)))
-
-    near = 1 - core
-    far = core
-
-    @pl.when(core == 0)
-    def _():
-        to_west.wait_recv()
-
-    @pl.when(core == 1)
-    def _():
-        to_east.wait_recv()
-
-    filter_side(near)
+                    spread[side, k, to : to + WINDOW] = result[k * WINDOW : (k + 1) * WINDOW]
+
+    def field_product(side, k, start, stop):
+        lhs = field[side, start:stop].reshape((stop - start) * side_cols, chans)
+        rhs = spread[side, k, start * side_cols : stop * side_cols]
+        return dot(lhs, rhs, ((0,), (0,)))
+
+    def add_product(k, start, stop):
+        result = field_product(far, k, start, stop)
+        part[0, k] += result[:, :lanes]
+        part[1, k] += result[:, lanes:]
+
+    near_copy(True).wait_recv()
+    near_at = columns(near * (cols + HALO), HALO)
+    pl.loop(1, rows + 1, unroll=4)(lambda row: scale_row(row, near_at))
+    filter_rows(near, 0, rows)
     loads[4].wait()
     loads[5].wait()
     for k in range(K):
-        result = field_product(near, k)
+        result = field_product(near, k, 0, rows)
         part[0, k] = result[:, :lanes]
         part[1, k] = result[:, lanes:]
 
-    @pl.when(core == 0)
-    def _():
-        to_east.wait_recv()
-
-    @pl.when(core == 1)
-    def _():
-        to_west.wait_recv()
-
-    filter_side(far)
+    far_at = columns(far * (cols + HALO), HALO)
+    for chunk in range(CHUNKS):
+        if chunk == CHUNKS - 1:
+            for k in range(K):
+                add_product(k, 0, rows // 2)
+        far_copy(chunk, True).wait_recv()
+        for row in range(1 + chunk * tall, 1 + (chunk + 1) * tall):
+            scale_row(row, far_at)
+        start = chunk * tall - 1 if chunk else 0
+        stop = (chunk + 1) * tall - 1 if chunk < CHUNKS - 1 else rows
+        filter_rows(far, start, stop)
 
     def pair_copy(group):
         ks = pl.ds(group * GROUP, GROUP)
@@ -313,12 +332,8 @@
 
     for group in range(GROUPS):
         for k in range(group * GROUP, (group + 1) * GROUP):
-            result = field_product(far, k)
-            part[0, k] += result[:, :lanes]
-            part[1, k] += result[:, lanes:]
+            add_product(k, rows // 2, rows)
         pair_copy(group).start()
-        if group > 0:
-            reduce_pair(group - 1)
 
     loads[6].wait()
 
@@ -327,26 +342,21 @@
         total = dot(spread[side, 0, at], weight[0], ((1,), (1,)))
         for k in range(1, K):
             total += dot(spread[side, k, at], weight[k], ((1,), (1,)))
-        tall = 256 // side_cols
-        to = pl.ds(block * tall, tall)
+        high = 256 // side_cols
+        to = pl.ds(block * high, high)
         grad_ref[to, side * side_cols : (side + 1) * side_cols] = total.reshape(
-            tall, side_cols, chans
+            high, side_cols, chans
         )
 
     blocks = [(side, block) for side in range(2) for block in range(side_spots // 256)]
-    share = -(-len(blocks) // 4)
-    for block in blocks[:share]:
-        grad_block(*block)
-    reduce_pair(GROUPS - 1)
-    for block in blocks[share : 2 * share]:
-        grad_block(*block)
-    reduce_lat(0)
-    for block in blocks[2 * share : 3 * share]:
-        grad_block(*block)
-    reduce_lat(1)
-    for block in blocks[3 * share :]:
-        grad_block(*block)
-    reduce_lat(2)
+    cuts = [len(blocks) * n // 8 for n in (0, 2, 3, 4, 8)]
+    for step in range(4):
+        for block in blocks[cuts[step] : cuts[step + 1]]:
+            grad_block(*block)
+        if step < GROUPS:
+            reduce_pair(step)
+    for group in range(GROUPS):
+        reduce_lat(group)
 
     def all_copy(k, step):
         return pltpu.make_async_remote_copy(
@@ -391,8 +401,9 @@
         for side in range(2):
             wgrad_ref[k, :, side * lanes : (side + 1) * lanes] = final[side, k].astype(F32)
 
-    to_east.wait_send()
-    to_west.wait_send()
+    near_copy(False).wait_send()
+    for chunk in range(CHUNKS):
+        far_copy(chunk, False).wait_send()
 
     @pl.when(has_down)
     def _():
@@ -436,13 +447,10 @@
     side_cols = cols // 2
     ext = cols + 2 * HALO
     size = 2 * HALO + 1
-    centres = np.arange(nlat, dtype=np.float32) + np.float32(0.5)
-    area = np.float32(np.pi / 2) * np.sin(np.float32(np.pi) * centres / np.float32(nlat))
     scale = 1.0 / math.sqrt(nlat * cols * n_lon)
     sizes = (n_lat, n_lon, rows, cols, chans, nlat, scale)
     whole = pl.BlockSpec(memory_space=pltpu.HBM)
     vmem = pl.BlockSpec(memory_space=pltpu.VMEM)
-    smem = pl.BlockSpec(memory_space=pltpu.SMEM)
     dma = pltpu.SemaphoreType.DMA
     table = pltpu.VMEM((3, nlat, 128), F32)
     return pl.pallas_call(
@@ -451,7 +459,7 @@
             pltpu.VMEM((rows, cols, chans), F32),
             pltpu.VMEM((K, wide, chans), F32),
         ),
-        in_specs=[whole] * 6 + [smem],
+        in_specs=[whole] * 6,
         out_specs=(vmem, vmem),
         scratch_shapes=[
             pltpu.VMEM((rows + 2, ext, chans), BF16),
@@ -461,6 +469,7 @@
             pltpu.VMEM((3, size, nlat), jnp.int32),
             pltpu.VMEM((1, nlat), jnp.int32),
             table, table,
+            pltpu.VMEM((-(-(rows + 2) // 8) * 8, 128), F32),
             pltpu.VMEM((rows, K * WINDOW, 256), BF16),
             pltpu.VMEM((2, K, rows * side_cols, chans), BF16),
             pltpu.VMEM((2, K, chans, lanes), F32),
@@ -470,7 +479,7 @@
             pltpu.VMEM((K, wide, lanes), F32),
             pltpu.VMEM((chips, wide, lanes), F32),
             pltpu.VMEM((2, K, wide, lanes), BF16),
-            dma((7,)), dma((8,)), dma((8,)), dma((GROUPS,)), dma((GROUPS,)),
+            dma((7,)), dma((11,)), dma((11,)), dma((GROUPS,)), dma((GROUPS,)),
             dma((GROUPS, n_lat)), dma((GROUPS, n_lat)), dma((K,)), dma((chips,)),
             dma((chips,)), dma((K,)), dma((K,)), dma((K,)),
         ],
@@ -482,9 +491,12 @@
             bytes_accessed=6 * 2**20, transcendentals=0,
         ),
     )(
-        cotangent, input_field, weight,
-        basis_values.transpose(1, 2, 0), basis_index.transpose(1, 2, 0),
-        halo_width.reshape(1, nlat), jnp.asarray(area),
+        *(
+            pltpu.with_memory_space_constraint(x, pltpu.HBM) for x in (
+            cotangent, input_field, weight,
+            basis_values.transpose(1, 2, 0), basis_index.transpose(1, 2, 0),
+            halo_width.reshape(1, nlat),
+        )),
     )
 
 

time: 67.1 us -> 61 us (0.909)
  local copies, waits for them, and re-layouts: 8.94 us -> 2.03 us
  Pallas kernels: 57.2 us -> 58.3 us
    unnamed x16 -> x2, local copies, waits for them, and re-layouts: 8.94 us -> 2.03 us
    pallas_call x1, Pallas kernels: 57.2 us -> 58.3 us  [shards(): pl.pallas_call(functools.partial(kernel, sizes), out_shape=(pltpu.VMEM((r...]
where the time goes in v2:
time: 61 us; the launch traced here: 60.9 us
  Pallas kernels  58.3 us (96%)
  local copies, waits for them, and re-layouts  2.03 us (3%)
  between operations  0.64 us (1%)
    pallas_call x1, Pallas kernels, shards(): pl.pallas_call(functools.partial(kernel, sizes), out_shape=(pltpu.VMEM((r...  58.3 us
    unnamed x2, local copies, waits for them, and re-layouts  2.03 us

profile of v2, /device:TPU:1, one launch (start us, length us, event | category | flops | bytes accessed | tf_op | source)
XLA Modules:
  0.0 60.9 jit_solution(13019896414769989266)
XLA Ops:
  0.6 58.3 %shard_map.77 = (f32[32,64,256]{2,1,0:T(8,128)S(1)}, f32[9,32,256]{2,1,0:T(8,128)S(1)}) custom-call(bf16[32,64,256]{2,1,0:T(8,128)(2,1)} %cot_hbm.1, bf16[32,64,256]{2,1,0:T(8,128)(2,1)} %field_hbm.1, bf16[9,256,256]{2,1,0:T(8,128)(2,1)} %weight_hbm.1, bf16[3,65,256]{2,1,0:T(8,128)(2,1)} %bitcast.4, s32[3,65,256]{2,1,0:T(8,128)} %bitcast.3, s32[1,256]{1,0:T(1,128)} %bitcast.5), custom_call_target="tpu_custom_call" | custom-call | flops 8455716864 | bytes 6291456 | tf_op jit(solution)/shard_map/pallas_call | solution.py:456
  58.9 1.3 %copy.10 = f32[32,64,256]{2,1,0:T(8,128)} copy(f32[32,64,256]{2,1,0:T(8,128)S(1)} %get-tuple-element.2) | data formatting | bytes 4194304
  60.2 0.7 %copy.11 = f32[9,32,256]{2,1,0:T(8,128)} copy(f32[9,32,256]{2,1,0:T(8,128)S(1)} %get-tuple-element.3) | data formatting | bytes 589824

commit v3 on v2

--- a/solution.py
+++ b/solution.py
@@ -32,7 +32,7 @@
     cot, field, weight, values, index, width, flip_v, flip_i, area, taps, spread,
     part, pair, half, lat_in, band, lon_in, final,
     load_sems, halo_send, halo_recv, pair_send, pair_recv, lat_send, lat_recv,
-    lon_send, lon_recv, all_send, all_recv, mate_send, mate_recv,
+    lon_send, lon_recv, all_send, all_recv,
 ):
     n_lat, n_lon, rows, cols, chans, nlat, scale = sizes
     side_cols = cols // 2
@@ -40,15 +40,20 @@
     chips = n_lon // 2
     wide = chans // n_lat
     lanes = chans // 2
+    ring = chips // 2
     lat = lax.axis_index("lat")
     lon = lax.axis_index("lon")
     core = lax.rem(lon, 2)
     chip = lax.div(lon, 2)
+    spot = lax.rem(chip, ring)
+    base = lon - lax.rem(lon, 2 * ring)
     has_up = lat > 0
     has_down = lat < n_lat - 1
     west = lax.rem(lon + n_lon - 1, n_lon)
     east = lax.rem(lon + 1, n_lon)
     mate = lon + 1 - 2 * core
+    far_lon = lax.rem(lon + n_lon - 1 + 2 * core, n_lon)
+    outside = jnp.logical_or(far_lon < base, far_lon >= base + 2 * ring)
 
     loads = [
         pltpu.make_async_copy(values_hbm, values, load_sems.at[0]),
@@ -77,8 +82,7 @@
         greet((target, west))
         greet((target, east))
 
-    greet((lat, west))
-    greet((lat, east))
+    pl.when(outside)(lambda: greet((lat, far_lon)))
     pl.when(has_up)(lambda: greet_corner(lat - 1))
     pl.when(has_down)(lambda: greet_corner(lat + 1))
 
@@ -90,8 +94,13 @@
     def _(step):
         greet((lat, lax.rem(lon + 2 * step, n_lon)))
 
+    @pl.loop(0, ring)
+    def _(step):
+        greet((lat, base + lax.rem(mate - base + 2 * step, 2 * ring)))
+
     corners = 2 * (has_up.astype(jnp.int32) + has_down.astype(jnp.int32))
-    pl.semaphore_wait(barrier, n_lat - 1 + chips - 1 + 2 + corners)
+    others = n_lat - 1 + chips - 1 + ring + outside.astype(jnp.int32)
+    pl.semaphore_wait(barrier, others + corners)
 
     def halo(slot, source, target, device):
         return pltpu.make_async_remote_copy(
@@ -102,7 +111,6 @@
 
     near = 1 - core
     far = core
-    far_lon = lax.rem(lon + n_lon - 1 + 2 * core, n_lon)
     tall = rows // CHUNKS
 
     def columns(start, count):
@@ -144,7 +152,6 @@
         halo(10, cot_hbm.at[first], cot.at[below, ext_mid], (lat - 1, lon)),
     ]
     far_copy(0, False).start()
-    near_copy(False).start()
 
     @pl.when(has_down)
     def _():
@@ -156,6 +163,7 @@
         for copy in up:
             copy.start()
 
+    near_copy(False).start()
     for chunk in range(1, CHUNKS):
         far_copy(chunk, False).start()
 
@@ -212,27 +220,6 @@
     loads[3].wait()
     pl.loop(1, rows + 1, unroll=4)(lambda row: scale_row(row, ext_mid))
 
-    @pl.when(has_up)
-    def _():
-        for copy in down:
-            copy.wait_recv()
-
-    @pl.when(has_down)
-    def _():
-        for copy in up:
-            copy.wait_recv()
-
-    @pl.when(jnp.logical_not(has_up))
-    def _():
-        cot[0] = jnp.zeros_like(cot[0])
-
-    @pl.when(jnp.logical_not(has_down))
-    def _():
-        cot[rows + 1] = jnp.zeros_like(cot[rows + 1])
-
-    scale_edge(0)
-    scale_edge(rows + 1)
-
     def filter_rows(side, start, stop):
         for row in range(start, stop):
             lhs = taps[row][:, :DEPTH]
@@ -257,7 +244,30 @@
     near_copy(True).wait_recv()
     near_at = columns(near * (cols + HALO), HALO)
     pl.loop(1, rows + 1, unroll=4)(lambda row: scale_row(row, near_at))
-    filter_rows(near, 0, rows)
+    filter_rows(near, 1, rows - 1)
+
+    @pl.when(has_up)
+    def _():
+        for copy in down:
+            copy.wait_recv()
+
+    @pl.when(has_down)
+    def _():
+        for copy in up:
+            copy.wait_recv()
+
+    @pl.when(jnp.logical_not(has_up))
+    def _():
+        cot[0] = jnp.zeros_like(cot[0])
+
+    @pl.when(jnp.logical_not(has_down))
+    def _():
+        cot[rows + 1] = jnp.zeros_like(cot[rows + 1])
+
+    scale_edge(0)
+    scale_edge(rows + 1)
+    filter_rows(near, 0, 1)
+    filter_rows(near, rows - 1, rows)
     loads[4].wait()
     loads[5].wait()
     for k in range(K):
@@ -295,14 +305,19 @@
             device_id=(peer, lon), device_id_type=MESH,
         )
 
-    def owner_of(k):
-        return (k * chips) // K
-
-    def lon_copy(k, step):
+    def lon_copy(k, half_ring):
+        owner = half_ring * ring + k % ring
+        return owner, pltpu.make_async_remote_copy(
+            src_ref=band.at[k], dst_ref=lon_in.at[k // ring, chip],
+            send_sem=lon_send.at[k, half_ring], recv_sem=lon_recv.at[k // ring, chip],
+            device_id=(lat, owner * 2 + core), device_id_type=MESH,
+        )
+
+    def lon_arrival(k, source):
         return pltpu.make_async_remote_copy(
-            src_ref=band.at[k], dst_ref=lon_in.at[step],
-            send_sem=lon_send.at[k], recv_sem=lon_recv.at[step],
-            device_id=(lat, owner_of(k) * 2 + core), device_id_type=MESH,
+            src_ref=band.at[k], dst_ref=lon_in.at[k // ring, source],
+            send_sem=lon_send.at[k, 0], recv_sem=lon_recv.at[k // ring, source],
+            device_id=(lat, source * 2 + core), device_id_type=MESH,
         )
 
     def reduce_pair(group):
@@ -324,11 +339,10 @@
             total = half[k, at].astype(F32)
             for step in range(1, n_lat):
                 total += lat_in[step, k].astype(F32)
-            band[k] = total
-
-            @pl.when(chip != owner_of(k))
-            def _():
-                lon_copy(k, lax.rem(owner_of(k) - chip + chips, chips)).start()
+            band[k] = total.astype(BF16)
+            for half_ring in range(2):
+                owner, copy = lon_copy(k, half_ring)
+                pl.when(chip != owner)(copy.start)
 
     for group in range(GROUPS):
         for k in range(group * GROUP, (group + 1) * GROUP):
@@ -361,45 +375,42 @@
     def all_copy(k, step):
         return pltpu.make_async_remote_copy(
             src_ref=final.at[core, k], dst_ref=final.at[core, k],
-            send_sem=all_send.at[step], recv_sem=all_recv.at[k],
-            device_id=(lat, lax.rem(lon + 2 * step, n_lon)), device_id_type=MESH,
-        )
-
-    def mate_copy(k):
+            send_sem=all_send.at[k // ring, step], recv_sem=all_recv.at[core, k],
+            device_id=(lat, base + lax.rem(lon - base + step, 2 * ring)),
+            device_id_type=MESH,
+        )
+
+    def all_arrival(k, half_core):
         return pltpu.make_async_remote_copy(
-            src_ref=final.at[core, k], dst_ref=final.at[core, k],
-            send_sem=mate_send.at[k], recv_sem=mate_recv.at[k],
-            device_id=(lat, mate), device_id_type=MESH,
+            src_ref=final.at[half_core, k], dst_ref=final.at[half_core, k],
+            send_sem=all_send.at[0, 0], recv_sem=all_recv.at[half_core, k],
+            device_id=(lat, base + 2 * (k % ring) + half_core), device_id_type=MESH,
         )
 
     for k in range(K):
-        @pl.when(chip == owner_of(k))
+        @pl.when(spot == k % ring)
         def _():
             @pl.loop(1, chips)
             def _(step):
-                lon_copy(k, step).wait_recv()
-
-            total = band[k]
+                lon_arrival(k, lax.rem(chip + step, chips)).wait_recv()
+
+            total = band[k].astype(F32)
             for step in range(1, chips):
-                total += lon_in[step]
+                total += lon_in[k // ring, lax.rem(chip + step, chips)].astype(F32)
             final[core, k] = (total * scale).astype(BF16)
 
-            @pl.loop(1, chips)
+            @pl.loop(1, 2 * ring)
             def _(step):
                 all_copy(k, step).start()
 
-            mate_copy(k).start()
-
     for k in range(K):
-        @pl.when(chip != owner_of(k))
-        def _():
-            all_copy(k, 0).wait_recv()
-            mate_copy(k).start()
-
-    for k in range(K):
-        mate_copy(k).wait_recv()
-        for side in range(2):
-            wgrad_ref[k, :, side * lanes : (side + 1) * lanes] = final[side, k].astype(F32)
+        for half_core in range(2):
+            @pl.when(jnp.logical_or(spot != k % ring, core != half_core))
+            def _():
+                all_arrival(k, half_core).wait_recv()
+
+            of_core = slice(half_core * lanes, (half_core + 1) * lanes)
+            wgrad_ref[k, :, of_core] = final[half_core, k].astype(F32)
 
     near_copy(False).wait_send()
     for chunk in range(CHUNKS):
@@ -423,15 +434,13 @@
             lat_copy(group, step).wait_send()
 
     for k in range(K):
-        mate_copy(k).wait_send()
-
-        @pl.when(chip != owner_of(k))
+        for half_ring in range(2):
+            owner, copy = lon_copy(k, half_ring)
+            pl.when(chip != owner)(copy.wait_send)
+
+        @pl.when(spot == k % ring)
         def _():
-            lon_copy(k, 0).wait_send()
-
-        @pl.when(chip == owner_of(k))
-        def _():
-            @pl.loop(1, chips)
+            @pl.loop(1, 2 * ring)
             def _(step):
                 all_copy(k, step).wait_send()
 
@@ -444,6 +453,8 @@
     chips = n_lon // 2
     wide = chans // n_lat
     lanes = chans // 2
+    ring = chips // 2
+    held = -(-K // ring)
     side_cols = cols // 2
     ext = cols + 2 * HALO
     size = 2 * HALO + 1
@@ -476,12 +487,12 @@
             pltpu.VMEM((K, chans, lanes), F32),
             pltpu.VMEM((K, chans, lanes), BF16),
             pltpu.VMEM((n_lat, K, wide, lanes), BF16),
-            pltpu.VMEM((K, wide, lanes), F32),
-            pltpu.VMEM((chips, wide, lanes), F32),
+            pltpu.VMEM((K, wide, lanes), BF16),
+            pltpu.VMEM((held, chips, wide, lanes), BF16),
             pltpu.VMEM((2, K, wide, lanes), BF16),
             dma((7,)), dma((11,)), dma((11,)), dma((GROUPS,)), dma((GROUPS,)),
-            dma((GROUPS, n_lat)), dma((GROUPS, n_lat)), dma((K,)), dma((chips,)),
-            dma((chips,)), dma((K,)), dma((K,)), dma((K,)),
+            dma((GROUPS, n_lat)), dma((GROUPS, n_lat)), dma((K, 2)), dma((held, chips)),
+            dma((held, 2 * ring)), dma((2, K)),
         ],
         compiler_params=pltpu.CompilerParams(
             collective_id=0, has_side_effects=True, vmem_limit_bytes=40 * 2**20

time: 61 us -> 54.3 us (0.89)
  Pallas kernels: 58.3 us -> 51.5 us
    pallas_call x1, Pallas kernels: 58.3 us -> 51.5 us  [shards(): pl.pallas_call(functools.partial(kernel, sizes), out_shape=(pltpu.VMEM((r...]
where the time goes in v3:
time: 54.3 us; the launch traced here: 54.2 us
  Pallas kernels  51.5 us (95%)
  local copies, waits for them, and re-layouts  2.03 us (4%)
  between operations  0.64 us (1%)
    pallas_call x1, Pallas kernels, shards(): pl.pallas_call(functools.partial(kernel, sizes), out_shape=(pltpu.VMEM((r...  51.5 us
    unnamed x2, local copies, waits for them, and re-layouts  2.03 us

profile of v3, /device:TPU:1, one launch (start us, length us, event | category | flops | bytes accessed | tf_op | source)
XLA Modules:
  0.0 54.2 jit_solution(12723312840108691928)
XLA Ops:
  0.6 51.5 %shard_map.77 = (f32[32,64,256]{2,1,0:T(8,128)S(1)}, f32[9,32,256]{2,1,0:T(8,128)S(1)}) custom-call(bf16[32,64,256]{2,1,0:T(8,128)(2,1)} %cot_hbm.1, bf16[32,64,256]{2,1,0:T(8,128)(2,1)} %field_hbm.1, bf16[9,256,256]{2,1,0:T(8,128)(2,1)} %weight_hbm.1, bf16[3,65,256]{2,1,0:T(8,128)(2,1)} %bitcast.4, s32[3,65,256]{2,1,0:T(8,128)} %bitcast.3, s32[1,256]{1,0:T(1,128)} %bitcast.5), custom_call_target="tpu_custom_call" | custom-call | flops 8455716864 | bytes 6291456 | tf_op jit(solution)/shard_map/pallas_call | solution.py:467
  52.2 1.3 %copy.10 = f32[32,64,256]{2,1,0:T(8,128)} copy(f32[32,64,256]{2,1,0:T(8,128)S(1)} %get-tuple-element.2) | data formatting | bytes 4194304
  53.5 0.7 %copy.11 = f32[9,32,256]{2,1,0:T(8,128)} copy(f32[9,32,256]{2,1,0:T(8,128)S(1)} %get-tuple-element.3) | data formatting | bytes 589824

commit v4 on v3

--- a/solution.py
+++ b/solution.py
@@ -151,7 +151,6 @@
         halo(9, cot_hbm.at[first, low], cot.at[below, ext_high], (lat - 1, west)),
         halo(10, cot_hbm.at[first], cot.at[below, ext_mid], (lat - 1, lon)),
     ]
-    far_copy(0, False).start()
 
     @pl.when(has_down)
     def _():
@@ -164,7 +163,7 @@
             copy.start()
 
     near_copy(False).start()
-    for chunk in range(1, CHUNKS):
+    for chunk in range(CHUNKS):
         far_copy(chunk, False).start()
 
     latitude = lax.broadcasted_iota(jnp.int32, area.shape, 0) + (lat * rows - 1)
@@ -246,32 +245,10 @@
     pl.loop(1, rows + 1, unroll=4)(lambda row: scale_row(row, near_at))
     filter_rows(near, 1, rows - 1)
 
-    @pl.when(has_up)
-    def _():
-        for copy in down:
-            copy.wait_recv()
-
-    @pl.when(has_down)
-    def _():
-        for copy in up:
-            copy.wait_recv()
-
-    @pl.when(jnp.logical_not(has_up))
-    def _():
-        cot[0] = jnp.zeros_like(cot[0])
-
-    @pl.when(jnp.logical_not(has_down))
-    def _():
-        cot[rows + 1] = jnp.zeros_like(cot[rows + 1])
-
-    scale_edge(0)
-    scale_edge(rows + 1)
-    filter_rows(near, 0, 1)
-    filter_rows(near, rows - 1, rows)
     loads[4].wait()
     loads[5].wait()
     for k in range(K):
-        result = field_product(near, k, 0, rows)
+        result = field_product(near, k, 1, rows - 1)
         part[0, k] = result[:, :lanes]
         part[1, k] = result[:, lanes:]
 
@@ -279,13 +256,52 @@
     for chunk in range(CHUNKS):
         if chunk == CHUNKS - 1:
             for k in range(K):
-                add_product(k, 0, rows // 2)
+                add_product(k, 1, rows // 2)
         far_copy(chunk, True).wait_recv()
         for row in range(1 + chunk * tall, 1 + (chunk + 1) * tall):
             scale_row(row, far_at)
-        start = chunk * tall - 1 if chunk else 0
-        stop = (chunk + 1) * tall - 1 if chunk < CHUNKS - 1 else rows
+        start = max(chunk * tall - 1, 1)
+        stop = (chunk + 1) * tall - 1
         filter_rows(far, start, stop)
+
+    @pl.when(has_up)
+    def _():
+        for copy in down:
+            copy.wait_recv()
+
+    @pl.when(has_down)
+    def _():
+        for copy in up:
+            copy.wait_recv()
+
+    @pl.when(jnp.logical_not(has_up))
+    def _():
+        cot[0] = jnp.zeros_like(cot[0])
+
+    @pl.when(jnp.logical_not(has_down))
+    def _():
+        cot[rows + 1] = jnp.zeros_like(cot[rows + 1])
+
+    scale_edge(0)
+    scale_edge(rows + 1)
+    for side in range(2):
+        filter_rows(side, 0, 1)
+        filter_rows(side, rows - 1, rows)
+
+    def add_edges(k):
+        ends = (0, rows - 1)
+        lhs = jnp.concatenate([field[side, row] for side in range(2) for row in ends], axis=0)
+        rhs = jnp.concatenate(
+            [
+                spread[side, k, row * side_cols : (row + 1) * side_cols]
+                for side in range(2)
+                for row in ends
+            ],
+            axis=0,
+        )
+        result = dot(lhs, rhs, ((0,), (0,)))
+        part[0, k] += result[:, :lanes]
+        part[1, k] += result[:, lanes:]
 
     def pair_copy(group):
         ks = pl.ds(group * GROUP, GROUP)
@@ -346,7 +362,8 @@
 
     for group in range(GROUPS):
         for k in range(group * GROUP, (group + 1) * GROUP):
-            add_product(k, rows // 2, rows)
+            add_product(k, rows // 2, rows - 1)
+            add_edges(k)
         pair_copy(group).start()
 
     loads[6].wait()

time: 54.3 us -> 50.1 us (0.923)
  Pallas kernels: 51.5 us -> 47.4 us
    pallas_call x1, Pallas kernels: 51.5 us -> 47.4 us  [shards(): pl.pallas_call(functools.partial(kernel, sizes), out_shape=(pltpu.VMEM((r...]
where the time goes in v4:
time: 50.1 us
  Pallas kernels  47.4 us (95%)
  local copies, waits for them, and re-layouts  2.03 us (4%)
  between operations  0.64 us (1%)
    pallas_call x1, Pallas kernels, shards(): pl.pallas_call(functools.partial(kernel, sizes), out_shape=(pltpu.VMEM((r...  47.4 us
    unnamed x2, local copies, waits for them, and re-layouts  2.03 us

profile of v4, /device:TPU:1, one launch (start us, length us, event | category | flops | bytes accessed | tf_op | source)
XLA Modules:
  0.0 50.1 jit_solution(7809379772831264138)
XLA Ops:
  0.6 47.4 %shard_map.77 = (f32[32,64,256]{2,1,0:T(8,128)S(1)}, f32[9,32,256]{2,1,0:T(8,128)S(1)}) custom-call(bf16[32,64,256]{2,1,0:T(8,128)(2,1)} %cot_hbm.1, bf16[32,64,256]{2,1,0:T(8,128)(2,1)} %field_hbm.1, bf16[9,256,256]{2,1,0:T(8,128)(2,1)} %weight_hbm.1, bf16[3,65,256]{2,1,0:T(8,128)(2,1)} %bitcast.4, s32[3,65,256]{2,1,0:T(8,128)} %bitcast.3, s32[1,256]{1,0:T(1,128)} %bitcast.5), custom_call_target="tpu_custom_call" | custom-call | flops 8455716864 | bytes 6291456 | tf_op jit(solution)/shard_map/pallas_call | solution.py:484
  48.0 1.3 %copy.10 = f32[32,64,256]{2,1,0:T(8,128)} copy(f32[32,64,256]{2,1,0:T(8,128)S(1)} %get-tuple-element.2) | data formatting | bytes 4194304
  49.3 0.7 %copy.11 = f32[9,32,256]{2,1,0:T(8,128)} copy(f32[9,32,256]{2,1,0:T(8,128)S(1)} %get-tuple-element.3) | data formatting | bytes 589824

commit v5 on v4

--- a/solution.py
+++ b/solution.py
@@ -462,6 +462,32 @@
                 all_copy(k, step).wait_send()
 
 
+def write_kernel(grad_ref, wgrad_ref, grad_hbm, wgrad_hbm, sems):
+    pieces = sems.shape[0] - 1
+    tall = grad_ref.shape[0] // pieces
+    copies = [pltpu.make_async_copy(wgrad_ref, wgrad_hbm, sems.at[pieces])]
+    for piece in range(pieces):
+        at = pl.ds(piece * tall, tall)
+        copies.append(pltpu.make_async_copy(grad_ref.at[at], grad_hbm.at[at], sems.at[piece]))
+    for copy in copies:
+        copy.start()
+    for copy in copies:
+        copy.wait()
+
+
+def write_out(grad, wgrad):
+    vmem = pl.BlockSpec(memory_space=pltpu.VMEM)
+    whole = pl.BlockSpec(memory_space=pltpu.HBM)
+    return pl.pallas_call(
+        write_kernel,
+        out_shape=tuple(jax.ShapeDtypeStruct(x.shape, x.dtype) for x in (grad, wgrad)),
+        in_specs=(vmem, vmem),
+        out_specs=(whole, whole),
+        scratch_shapes=[pltpu.SemaphoreType.DMA((5,))],
+        compiler_params=pltpu.CompilerParams(vmem_limit_bytes=8 * 2**20),
+    )(*(pltpu.with_memory_space_constraint(x, pltpu.VMEM) for x in (grad, wgrad)))
+
+
 def shards(input_field, cotangent, weight, basis_values, basis_index, halo_width):
     n_lat = lax.axis_size("lat")
     n_lon = lax.axis_size("lon")
@@ -481,7 +507,7 @@
     vmem = pl.BlockSpec(memory_space=pltpu.VMEM)
     dma = pltpu.SemaphoreType.DMA
     table = pltpu.VMEM((3, nlat, 128), F32)
-    return pl.pallas_call(
+    grad, wgrad = pl.pallas_call(
         functools.partial(kernel, sizes),
         out_shape=(
             pltpu.VMEM((rows, cols, chans), F32),
@@ -526,6 +552,7 @@
             halo_width.reshape(1, nlat),
         )),
     )
+    return write_out(grad, wgrad)
 
 
 def solution(mesh):

time: 50.1 us -> 49.6 us (0.990)
  local copies, waits for them, and re-layouts: 2.03 us -> 0 us
  Pallas kernels: 47.4 us -> 48.8 us
    unnamed x2 -> x0, local copies, waits for them, and re-layouts: 2.03 us -> none
    pallas_call x0 -> x1, Pallas kernels: none -> 1.45 us  [write_out(): pl.pallas_call(write_kernel, out_shape=tuple((jax.ShapeDtypeStruct(x.shap...]
where the time goes in v5:
time: 49.6 us; the launch traced here: 49.5 us
  Pallas kernels  48.8 us (98%)
  between operations  0.64 us (1%)
    pallas_call x1, Pallas kernels, shards(): pl.pallas_call(functools.partial(kernel, sizes), out_shape=(pltpu.VMEM((r...  47.4 us
    pallas_call x1, Pallas kernels, write_out(): pl.pallas_call(write_kernel, out_shape=tuple((jax.ShapeDtypeStruct(x.shap...  1.45 us

profile of v5, /device:TPU:1, one launch (start us, length us, event | category | flops | bytes accessed | tf_op | source)
XLA Modules:
  0.0 49.5 jit_solution(1234347515777776425)
XLA Ops:
  0.6 47.4 %shard_map.77 = (f32[32,64,256]{2,1,0:T(8,128)S(1)}, f32[9,32,256]{2,1,0:T(8,128)S(1)}) custom-call(bf16[32,64,256]{2,1,0:T(8,128)(2,1)} %cot_hbm.1, bf16[32,64,256]{2,1,0:T(8,128)(2,1)} %field_hbm.1, bf16[9,256,256]{2,1,0:T(8,128)(2,1)} %weight_hbm.1, bf16[3,65,256]{2,1,0:T(8,128)(2,1)} %bitcast.4, s32[3,65,256]{2,1,0:T(8,128)} %bitcast.3, s32[1,256]{1,0:T(1,128)} %bitcast.5), custom_call_target="tpu_custom_call" | custom-call | flops 8455716864 | bytes 6291456 | tf_op jit(solution)/shard_map/pallas_call | solution.py:510
  48.0 1.5 %shard_map.78 = (f32[32,64,256]{2,1,0:T(8,128)}, f32[9,32,256]{2,1,0:T(8,128)}) custom-call(f32[32,64,256]{2,1,0:T(8,128)S(1)} %get-tuple-element.4.grad_ref, f32[9,32,256]{2,1,0:T(8,128)S(1)} %get-tuple-element.5.wgrad_ref), custom_call_target="tpu_custom_call" | custom-call | tf_op jit(solution)/shard_map/pallas_call | solution.py:481
